TPU v7x, 128 devices: a whole 4x4x4 slice. The times are simulated.
128 devices in a mesh: row: 16 (over y_hi, x, core), col: 8 (over z, y_lo).
Axes of the slice: x: 4, y: 4 (y_hi: 2, y_lo: 2; y = y_hi * 2 + y_lo), z: 4, core: 2. Of those that a mesh axis runs over, the one named last changes fastest.
Arguments:
- cycle_inter: float32 [1536, 1536, 128], P(None, ('row', 'col')), may hold values from -6 to 6
- integrals: float32 [1536, 1536, 128], P(None, ('row', 'col')), may hold values from -0.005859375 to 0.005859375
Outputs:
- ladder: float32 [128, 128], P('row')
All inputs are finite; a program needn't handle non-finite values.
Results may differ from a plain program's by a relative error of at most 0.0003.
Values sent between devices are 32-bit elements; how exact they have to be, the bound alone decides.
No kernel may reach another device: no remote copies, remote signals or barrier semaphores. Data moves between devices by JAX's collectives and lax.ppermute only.
A program may use at most 128 MiB of HBM per device.

v0:
```python
import jax
import jax.numpy as jnp
from jax import lax
from jax.sharding import PartitionSpec as P


def body(cycle_inter, integrals):
    row_count = lax.axis_size("row")
    col_count = lax.axis_size("col")
    local_width = cycle_inter.shape[1]
    occupied = cycle_inter.shape[2]
    slab_pairs = integrals.shape[2]
    received = lax.all_to_all(cycle_inter, ("row", "col"), split_axis=0, concat_axis=1, tiled=True)
    amplitudes = cycle_inter - jnp.swapaxes(received, 0, 1)
    device_rank = lax.axis_index("row") * col_count + lax.axis_index("col")
    first_column = device_rank * local_width
    column_ids = first_column + jnp.arange(local_width, dtype=jnp.int32)
    block_rows = 128
    needed_blocks = (first_column + local_width + block_rows - 1) // block_rows

    def accumulate(block_index, summed):
        offset = block_index * block_rows
        amp_block = lax.dynamic_slice_in_dim(amplitudes, offset, block_rows, 0)
        integral_block = lax.dynamic_slice_in_dim(integrals, offset, block_rows, 0)
        row_ids = offset + jnp.arange(block_rows, dtype=jnp.int32)
        upper_mask = (row_ids[:, None] < column_ids[None, :]).astype(jnp.float32)
        amp_block = amp_block * upper_mask[:, :, None]
        return summed + jnp.einsum(
            "cdi,cda->ia", amp_block, integral_block, precision=lax.Precision.HIGHEST
        )

    partial_sum = lax.fori_loop(
        0, needed_blocks, accumulate, jnp.zeros((occupied, slab_pairs), jnp.float32)
    )
    owned_rows = occupied // row_count
    summed = lax.psum(partial_sum, ("row", "col"))
    return lax.dynamic_slice_in_dim(summed, lax.axis_index("row") * owned_rows, owned_rows, 0)


def solution(mesh):
    return jax.shard_map(
        body,
        mesh=mesh,
        in_specs=(P(None, ("row", "col"), None), P(None, ("row", "col"), None)),
        out_specs=P("row", None),
        check_vma=False,
    )
```

profile of v0, /device:TPU:1, one launch (start us, length us, event | category | flops | bytes accessed | tf_op | source)
XLA Modules:
  0.0 412.1 jit_solution(1875631772332710024)
XLA Ops:
  6.5 12.7 %copy.7 = f32[1536,12,128]{2,1,0:T(8,128)} copy(f32[1536,12,128]{2,0,1:T(8,128)} %param.4) | data formatting | bytes 18874368 | tf_op args[0]
  19.2 11.9 %all-to-all-start = ((f32[1536,12,128]{2,1,0:T(8,128)}), f32[1536,12,128]{2,1,0:T(8,128)}, u32[]{:S(2)}, u32[]{:S(2)}) async-start(f32[1536,12,128]{2,1,0:T(8,128)} %copy.7), calls=%async_computation | async-start | bytes 25165824 | tf_op jit(solution)/shard_map/all_to_all | solution.py:13
  31.1 0.0 all-reduce.2.cloned.1.call-start
  31.2 165.2 %all-to-all-done = f32[1536,12,128]{2,1,0:T(8,128)} async-done(((f32[1536,12,128]{2,1,0:T(8,128)}), f32[1536,12,128]{2,1,0:T(8,128)}, u32[]{:S(2)}, u32[]{:S(2)}) %all-to-all-start) | async-done | bytes 9437216 | tf_op jit(solution)/shard_map/all_to_all | solution.py:13
  196.3 10.3 %copy.9 = f32[12,128,12,128]{3,2,1,0:T(8,128)} copy(f32[12,128,12,128]{3,2,0,1:T(8,128)} %bitcast.2) | data formatting | bytes 18874368 | tf_op jit(solution)/shard_map/all_to_all | solution.py:13
  206.7 12.0 %all_to_all.16 = f32[12,1536,128]{2,1,0:T(8,128)} reshape(f32[12,128,12,128]{3,2,1,0:T(8,128)} %copy.9) | data formatting | bytes 18874368 | tf_op jit(solution)/shard_map/all_to_all | solution.py:13
  218.7 10.9 %bitcast_subtract_fusion = f32[1536,12,128]{2,0,1:T(8,128)} fusion(f32[1536,12,128]{2,0,1:T(8,128)} %param.4, f32[12,1536,128]{2,1,0:T(8,128)} %all_to_all.16), kind=kLoop, calls=%fused_computation.11 | loop fusion | flops 2359296 | bytes 28311552 | tf_op jit(solution)/shard_map/sub | solution.py:14
  229.6 3.6 while.11
  229.6 1.2 constant_dynamic-slice_fusion.3
  230.8 0.3 copy.15
  231.1 0.1 compare_convert_fusion.2
  231.2 2.1 fusion.12
  233.2 0.0 copy-start
  233.2 0.6 copy-done
  233.9 0.0 all-reduce.2.cloned.1.call-update
  233.9 170.1 %all-reduce.2.cloned.1.call-done = f32[128,128]{1,0:T(8,128)} async-done(((f32[128,128]{1,0:T(8,128)}), f32[128,128]{1,0:T(8,128)}) %all-reduce.2.cloned.1.call-update) | async-done | bytes 65552 | tf_op jit(solution)/shard_map/psum | solution.py:36
  404.0 1.3 constant_dynamic-slice_fusion.1
  (3 shorter events, 0.0 us)
Async XLA Ops:
  19.2 177.2 %all-to-all-start = ((f32[1536,12,128]{2,1,0:T(8,128)}), f32[1536,12,128]{2,1,0:T(8,128)}, u32[]{:S(2)}, u32[]{:S(2)}) async-start(f32[1536,12,128]{2,1,0:T(8,128)} %copy.7), calls=%async_computation | async-start | bytes 25165824 | tf_op jit(solution)/shard_map/all_to_all | solution.py:13
  31.1 372.9 %all-reduce.2.cloned.1.call-start = ((), (), s32[]{:S(2)}) async-start(), calls=%async_computation.1 | async-start | bytes 131072 | tf_op jit(solution)/shard_map/psum | solution.py:36
  233.2 0.6 copy-start
Sparse Core Ops, SparseCore 0:
  234.0 169.9 all-reduce.1
where the time goes:
time: 414 us; the launch traced here: 412 us
  waiting for transfers between devices  335 us (81%)
  local copies, waits for them, and re-layouts  38.3 us (9%)
  between operations  13.4 us (3%)
  starting transfers between devices  11.9 us (3%)
  other arithmetic  11 us (3%)
    psum x1, waiting for transfers between devices, body(): summed = lax.psum(partial_sum, ('row', 'col'))  170 us
    all_to_all x1, waiting for transfers between devices, body(): lax.all_to_all(cycle_inter, ('row', 'col'), split_axis=0, concat_axis=1,...  165 us
    all_to_all x2, local copies, waits for them, and re-layouts, body(): lax.all_to_all(cycle_inter, ('row', 'col'), split_axis=0, concat_axis=1,...  22.3 us
    unnamed x3, local copies, waits for them, and re-layouts  13.3 us
    all_to_all x1, starting transfers between devices, body(): lax.all_to_all(cycle_inter, ('row', 'col'), split_axis=0, concat_axis=1,...  11.9 us
    sub x1, other arithmetic, body(): amplitudes = cycle_inter - jnp.swapaxes(received, 0, 1)  10.9 us
  transfers between devices with their start and end apart: 2, of which 2 were waited for; matrix products, arithmetic and copies ran while one was open for 0% of the time, Pallas kernels for 0%

commit v1 on v0

--- a/solution.py
+++ b/solution.py
@@ -33,7 +33,9 @@
         0, needed_blocks, accumulate, jnp.zeros((occupied, slab_pairs), jnp.float32)
     )
     owned_rows = occupied // row_count
-    summed = lax.psum(partial_sum, ("row", "col"))
+    summed = partial_sum
+    for i in ("row", "col"):
+        summed = lax.psum(summed, axis_name=i)
     return lax.dynamic_slice_in_dim(summed, lax.axis_index("row") * owned_rows, owned_rows, 0)
 
 

time: 414 us -> 478 us (1.15)
  waiting for transfers between devices: 335 us -> 395 us
    psum x1 -> x2, waiting for transfers between devices: 170 us -> 230 us  [body(): summed = lax.psum(summed, axis_name=i)]
  transfers between devices with their start and end apart: 2 -> 3, of which waited for: 2 -> 3; matrix products, arithmetic and copies ran while one was open for 0% -> 0% of each run, Pallas kernels for 0% -> 0%
where the time goes in v1:
time: 478 us; the launch traced here: 472 us
  waiting for transfers between devices  395 us (83%)
  local copies, waits for them, and re-layouts  38.3 us (8%)
  between operations  13.4 us (3%)
  starting transfers between devices  12 us (3%)
  other arithmetic  11 us (2%)
    psum x2, waiting for transfers between devices, body(): summed = lax.psum(summed, axis_name=i)  230 us
    all_to_all x1, waiting for transfers between devices, body(): lax.all_to_all(cycle_inter, ('row', 'col'), split_axis=0, concat_axis=1,...  165 us
    all_to_all x2, local copies, waits for them, and re-layouts, body(): lax.all_to_all(cycle_inter, ('row', 'col'), split_axis=0, concat_axis=1,...  22.3 us
    unnamed x3, local copies, waits for them, and re-layouts  13.3 us
    all_to_all x1, starting transfers between devices, body(): lax.all_to_all(cycle_inter, ('row', 'col'), split_axis=0, concat_axis=1,...  11.9 us
    sub x1, other arithmetic, body(): amplitudes = cycle_inter - jnp.swapaxes(received, 0, 1)  10.9 us
  transfers between devices with their start and end apart: 3, of which 3 were waited for; matrix products, arithmetic and copies ran while one was open for 0% of the time, Pallas kernels for 0%

profile of v1, /device:TPU:1, one launch (start us, length us, event | category | flops | bytes accessed | tf_op | source)
XLA Modules:
  0.0 471.9 jit_solution(12249380873708650889)
XLA Ops:
  6.5 12.7 %copy.7 = f32[1536,12,128]{2,1,0:T(8,128)} copy(f32[1536,12,128]{2,0,1:T(8,128)} %param.4) | data formatting | bytes 18874368 | tf_op args[0]
  19.2 11.9 %all-to-all-start = ((f32[1536,12,128]{2,1,0:T(8,128)}), f32[1536,12,128]{2,1,0:T(8,128)}, u32[]{:S(2)}, u32[]{:S(2)}) async-start(f32[1536,12,128]{2,1,0:T(8,128)} %copy.7), calls=%async_computation | async-start | bytes 25165824 | tf_op jit(solution)/shard_map/all_to_all | solution.py:13
  31.1 0.0 all-reduce.3.cloned.1.call-start
  31.2 165.2 %all-to-all-done = f32[1536,12,128]{2,1,0:T(8,128)} async-done(((f32[1536,12,128]{2,1,0:T(8,128)}), f32[1536,12,128]{2,1,0:T(8,128)}, u32[]{:S(2)}, u32[]{:S(2)}) %all-to-all-start) | async-done | bytes 9437216 | tf_op jit(solution)/shard_map/all_to_all | solution.py:13
  196.3 10.3 %copy.9 = f32[12,128,12,128]{3,2,1,0:T(8,128)} copy(f32[12,128,12,128]{3,2,0,1:T(8,128)} %bitcast.2) | data formatting | bytes 18874368 | tf_op jit(solution)/shard_map/all_to_all | solution.py:13
  206.7 12.0 %all_to_all.16 = f32[12,1536,128]{2,1,0:T(8,128)} reshape(f32[12,128,12,128]{3,2,1,0:T(8,128)} %copy.9) | data formatting | bytes 18874368 | tf_op jit(solution)/shard_map/all_to_all | solution.py:13
  218.7 10.9 %bitcast_subtract_fusion = f32[1536,12,128]{2,0,1:T(8,128)} fusion(f32[1536,12,128]{2,0,1:T(8,128)} %param.4, f32[12,1536,128]{2,1,0:T(8,128)} %all_to_all.16), kind=kLoop, calls=%fused_computation.11 | loop fusion | flops 2359296 | bytes 28311552 | tf_op jit(solution)/shard_map/sub | solution.py:14
  229.6 3.6 while.11
  229.6 1.2 constant_dynamic-slice_fusion.3
  230.8 0.3 copy.15
  231.1 0.1 compare_convert_fusion.2
  231.2 2.1 fusion.12
  233.2 0.0 copy-start
  233.2 0.6 copy-done
  233.9 0.0 all-reduce.3.cloned.1.call-update
  233.9 0.0 all-reduce.5.cloned.1.call-start
  233.9 158.1 %all-reduce.3.cloned.1.call-done = f32[128,128]{1,0:T(8,128)} async-done(((f32[128,128]{1,0:T(8,128)}), f32[128,128]{1,0:T(8,128)}) %all-reduce.3.cloned.1.call-update) | async-done | bytes 65552 | tf_op jit(solution)/shard_map/psum | solution.py:38
  392.1 0.0 all-reduce.5.cloned.1.call-update
  392.1 71.7 %all-reduce.5.cloned.1.call-done = f32[128,128]{1,0:T(8,128)} async-done(((f32[128,128]{1,0:T(8,128)}), f32[128,128]{1,0:T(8,128)}) %all-reduce.5.cloned.1.call-update) | async-done | bytes 65552 | tf_op jit(solution)/shard_map/psum | solution.py:38
  463.8 1.3 constant_dynamic-slice_fusion.1
  (3 shorter events, 0.0 us)
Async XLA Ops:
  19.2 177.2 %all-to-all-start = ((f32[1536,12,128]{2,1,0:T(8,128)}), f32[1536,12,128]{2,1,0:T(8,128)}, u32[]{:S(2)}, u32[]{:S(2)}) async-start(f32[1536,12,128]{2,1,0:T(8,128)} %copy.7), calls=%async_computation | async-start | bytes 25165824 | tf_op jit(solution)/shard_map/all_to_all | solution.py:13
  31.1 361.0 %all-reduce.3.cloned.1.call-start = ((), (), s32[]{:S(2)}) async-start(), calls=%async_computation.1 | async-start | bytes 131072 | tf_op jit(solution)/shard_map/psum | solution.py:38
  233.2 0.6 copy-start
  233.9 229.9 %all-reduce.5.cloned.1.call-start = ((), (), s32[]{:S(2)}) async-start(), calls=%async_computation.2 | async-start | bytes 131072 | tf_op jit(solution)/shard_map/psum | solution.py:38
Sparse Core Ops, SparseCore 0:
  234.0 158.0 all-reduce.2
  394.7 69.0 all-reduce.4
